TPU v7x, 256 devices: a whole 4x4x8 slice. The times are simulated.
256 devices in a mesh: blk: 32 (over z, x_hi, core), tensor: 8 (over y, x_lo).
Axes of the slice: x: 4 (x_hi: 2, x_lo: 2; x = x_hi * 2 + x_lo), y: 4, z: 8, core: 2. Of those that a mesh axis runs over, the one named last changes fastest.
Arguments:
- queries: bfloat16 [16384, 2048], P('blk', 'tensor'), may hold values from -5 to 5
- key_states: bfloat16 [16384, 2048], P('blk', 'tensor'), may hold values from -5 to 5
- value_states: bfloat16 [16384, 2048], P('blk', 'tensor'), may hold values from -6 to 6
- out_weight: bfloat16 [2048, 4096], P('tensor'), may hold values from -0.1875 to 0.1875
- lengths: int32 [32], replicated, may hold values from 128 to 512, as said below
- cycle_order: int32 [32], replicated, may hold values from 0 to 31, each once
Outputs:
- mixed_out: bfloat16 [16384, 4096], P('blk', 'tensor')
Inputs may be any that keep to these rules, and one draw needn't show every extreme that they name: lengths are multiples of 128; some slice is full and some holds exactly 128 tokens. `cycle_order`: each slice number appears once.
All inputs are finite; a program needn't handle non-finite values.
Results may differ from a plain program's by a relative error of at most 0.009.
Values may be sent and summed in bfloat16 or wider, within the bound.
A program may use at most 128 MiB of HBM per device.

v0:
```python
import jax
import jax.numpy as jnp
from jax import lax
from jax.sharding import PartitionSpec as P

HD = 128


NEG_FILL = -1e30
BLOCK_ROWS = 512


def slice_starts(lengths, cycle_order):
    before = (cycle_order[None, :] < cycle_order[:, None]).astype(jnp.int32)
    return jnp.sum(before * lengths[None, :], axis=1)


def lookup(lookup_table, wanted):
    slot_ids = jnp.arange(lookup_table.shape[0], dtype=jnp.int32)
    return jnp.sum(
        jnp.where(wanted[:, None] == slot_ids[None, :], lookup_table[None, :], 0), axis=1
    )


def place(starts, lengths, first_row, row_count, capacity):
    row_index = first_row + jnp.arange(row_count, dtype=jnp.int32)
    holder = row_index // capacity
    offset = row_index % capacity
    return (lookup(starts, holder) + offset, offset < lookup(lengths, holder))


def attend_tile(
    carried, query_heads, query_pos, query_valid, key_rows, value_rows, key_pos, key_valid
):
    head_count = query_heads.shape[1]
    key_heads = key_rows.reshape(key_rows.shape[0], head_count, HD)
    value_heads = value_rows.reshape(value_rows.shape[0], head_count, HD)
    allowed = (
        query_valid[:, None] & key_valid[None, :] & (key_pos[None, :] <= query_pos[:, None])
    )[None]
    accumulator, running_max, running_sum = carried
    scores = jnp.einsum(
        "qhd,khd->hqk", query_heads, key_heads, preferred_element_type=jnp.float32
    ) * HD ** (-0.5)
    masked = jnp.where(allowed, scores, NEG_FILL)
    new_max = jnp.maximum(running_max, jnp.max(masked, axis=2))
    rescale = jnp.exp(running_max - new_max)
    weights = jnp.where(allowed, jnp.exp(masked - new_max[..., None]), 0.0)
    new_sum = running_sum * rescale + jnp.sum(weights, axis=2)
    update = jnp.einsum(
        "hqk,khd->hqd",
        weights.astype(jnp.bfloat16),
        value_heads,
        preferred_element_type=jnp.float32,
    )
    return (accumulator * rescale[..., None] + update, new_max, new_sum)


def body(queries, key_states, value_states, out_weight, lengths, cycle_order):
    capacity = queries.shape[0]
    head_count = queries.shape[1] // HD
    own_index = lax.axis_index("blk")
    starts = slice_starts(lengths, cycle_order)
    own_pos, own_valid = place(starts, lengths, own_index * capacity, capacity, capacity)
    query_heads = queries.reshape(capacity, head_count, HD)
    initial = (
        jnp.zeros((head_count, capacity, HD), jnp.float32),
        jnp.full((head_count, capacity), NEG_FILL, jnp.float32),
        jnp.zeros((head_count, capacity), jnp.float32),
    )
    carried = initial
    key_rows = lax.all_gather(key_states, "blk", axis=0, tiled=True)
    value_rows = lax.all_gather(value_states, "blk", axis=0, tiled=True)
    row_count = key_rows.shape[0]
    key_pos, key_valid = place(starts, lengths, jnp.int32(0), row_count, capacity)
    splits = row_count // BLOCK_ROWS

    def visit_block(inner_carry, block_data):
        block_keys, block_values, block_pos, block_valid = block_data
        return (
            attend_tile(
                inner_carry,
                query_heads,
                own_pos,
                own_valid,
                block_keys,
                block_values,
                block_pos,
                block_valid,
            ),
            None,
        )

    block_stack = (
        key_rows.reshape(splits, BLOCK_ROWS, key_rows.shape[1]),
        value_rows.reshape(splits, BLOCK_ROWS, value_rows.shape[1]),
        key_pos.reshape(splits, BLOCK_ROWS),
        key_valid.reshape(splits, BLOCK_ROWS),
    )
    carried, leftover = lax.scan(visit_block, carried, block_stack)
    accumulator, running_max, running_sum = carried
    safe_sum = jnp.where(own_valid[None, :], running_sum, 1.0)
    attended = jnp.where(own_valid[None, :, None], accumulator / safe_sum[..., None], 0.0).astype(
        jnp.bfloat16
    )
    partial_value = jnp.einsum(
        "hqd,hde->qe",
        attended,
        out_weight.reshape(head_count, HD, out_weight.shape[1]),
        preferred_element_type=jnp.float32,
    )
    return lax.psum_scatter(partial_value, "tensor", scatter_dimension=1, tiled=True).astype(
        jnp.bfloat16
    )


def solution(mesh):
    placed = (
        P("blk", "tensor"),
        P("blk", "tensor"),
        P("blk", "tensor"),
        P("tensor", None),
        P(),
        P(),
    )
    return jax.shard_map(
        body, mesh=mesh, in_specs=placed, out_specs=P("blk", "tensor"), check_vma=False
    )
```

profile of v0, /device:TPU:1, one launch (start us, length us, event | category | flops | bytes accessed | tf_op | source)
XLA Modules:
  0.0 554.7 jit_solution(16705595512832779738)
XLA Ops:
  9.0 1.4 select_reduce_fusion
  12.0 103.8 %all-gather.3.cloned.1.call-done = bf16[16384,256]{1,0:T(8,128)(2,1)} async-done(((bf16[512,256]{1,0:T(8,128)(2,1)}), bf16[16384,256]{1,0:T(8,128)(2,1)}) %all-gather.3.cloned.1.call-update) | async-done | bytes 8388624 | tf_op jit(solution)/shard_map/all_gather | solution.py:72
  115.8 100.8 %all-gather.5.cloned.1.call-done = bf16[16384,256]{1,0:T(8,128)(2,1)} async-done(((bf16[512,256]{1,0:T(8,128)(2,1)}), bf16[16384,256]{1,0:T(8,128)(2,1)}) %all-gather.5.cloned.1.call-update) | async-done | bytes 8388624 | tf_op jit(solution)/shard_map/all_gather | solution.py:73
  216.6 155.8 %while.15 = (s32[]{:T(128)}, f32[2,512,128]{2,1,0:T(8,128)}, f32[2,512]{1,0:T(2,128)S(1)}, f32[2,512]{1,0:T(2,128)S(1)}, pred[512]{0:T(512)(128)(4,1)S(1)}, /*in...) while((s32[]{:T(128)}, f32[2,512,128]{2,1,0:T(8,128)}, ...), condition=%wide.region_8.9_spmd.clone, body=%wide.region_5.8_spmd.clone.sunk | while | flops 276435968 | bytes 15542485 | solution.py:100
  219.6 1.1 convolution_add_fusion.2
  224.4 1.1 convolution_add_fusion.2
  229.3 1.1 convolution_add_fusion.2
  234.2 1.1 convolution_add_fusion.2
  239.0 1.1 convolution_add_fusion.2
  243.9 1.1 convolution_add_fusion.2
  248.8 1.1 convolution_add_fusion.2
  253.6 1.1 convolution_add_fusion.2
  258.5 1.1 convolution_add_fusion.2
  263.4 1.1 convolution_add_fusion.2
  268.2 1.1 convolution_add_fusion.2
  273.1 1.1 convolution_add_fusion.2
  278.0 1.1 convolution_add_fusion.2
  282.8 1.1 convolution_add_fusion.2
  287.7 1.1 convolution_add_fusion.2
  292.6 1.1 convolution_add_fusion.2
  297.5 1.1 convolution_add_fusion.2
  372.4 5.7 %convolution_bitcast_fusion = f32[512,4096]{1,0:T(8,128)} fusion(bf16[2,128,4096]{2,1,0:T(8,128)(2,1)S(1)} %bitcast.42, f32[2,512,128]{2,1,0:T(8,128)} %get-tuple-element.63, f32[2,512]{1,0:T(2,128)S(1)} %broadcast_select_fusion.1, pred[512]{0:T(512)(128)(4,1)S(1)} %get-tuple-element.296), kind=kOutput, calls=%fused_computation.24 | convolution fusion | flops 1074135040 | bytes 11014656 | tf_op jit(solution)/shard_map/hqd,hde->qe/dot_general | solution.py:106
  378.1 168.0 %reduce-scatter.2.cloned.1.call-done = f32[512,512]{1,0:T(8,128)} async-done(((f32[512,4096]{1,0:T(8,128)}), f32[512,512]{1,0:T(8,128)}) %reduce-scatter.2.cloned.1.call-update) | async-done | bytes 1048592 | tf_op jit(solution)/shard_map/reduce_scatter | solution.py:112
  546.1 2.1 convert_element_type.11
  (521 shorter events, 138.3 us)
Async XLA Ops:
  6.5 365.8 %copy-start = (bf16[256,4096]{1,0:T(8,128)(2,1)S(1)}, bf16[256,4096]{1,0:T(8,128)(2,1)}, u32[]{:S(2)}) copy-start(bf16[256,4096]{1,0:T(8,128)(2,1)} %param.11) | copy-start | bytes 6291460
  6.5 5.2 copy-start.3
  6.5 109.3 %all-gather.3.cloned.1.call-start = ((), (), s32[]{:S(2)}) async-start(), calls=%async_computation.1 | async-start | bytes 8650752 | tf_op jit(solution)/shard_map/all_gather | solution.py:72
  7.3 209.3 %all-gather.5.cloned.1.call-start = ((), (), s32[]{:S(2)}) async-start(), calls=%async_computation.2 | async-start | bytes 8650752 | tf_op jit(solution)/shard_map/all_gather | solution.py:73
  8.0 538.1 %reduce-scatter.2.cloned.1.call-start = ((), (), s32[]{:S(2)}) async-start(), calls=%async_computation.3 | async-start | bytes 9437184 | tf_op jit(solution)/shard_map/reduce_scatter | solution.py:112
  218.3 1.3 copy-start.1
  223.2 1.3 copy-start.1
  228.0 1.3 copy-start.1
  232.9 1.3 copy-start.1
  237.8 1.3 copy-start.1
  242.6 1.3 copy-start.1
  247.5 1.3 copy-start.1
  252.4 1.3 copy-start.1
  257.2 1.3 copy-start.1
  262.1 1.3 copy-start.1
  267.0 1.3 copy-start.1
  271.8 1.3 copy-start.1
  276.7 1.3 copy-start.1
  281.6 1.3 copy-start.1
  291.3 1.3 copy-start.1
  305.9 1.3 copy-start.1
  315.7 1.3 copy-start.1
  340.0 1.3 copy-start.1
  349.7 1.3 copy-start.1
  (45 other events, 41.9 us)
Sparse Core Ops, SparseCore 0:
  10.1 105.6 all-gather.2
  118.6 97.9 all-gather.4
  378.2 167.8 reduce-scatter.1
where the time goes:
time: 556 us; the launch traced here: 555 us
  waiting for transfers between devices  374 us (67%)
  local copies, waits for them, and re-layouts  70.8 us (13%)
  matrix products  61.5 us (11%)
  other arithmetic  32.5 us (6%)
  between operations  13.2 us (2%)
    reduce_scatter x1, waiting for transfers between devices, body(): lax.psum_scatter(partial_value, 'tensor', scatter_dimension=1, tiled=True)  168 us
    all_gather x1, waiting for transfers between devices, body(): key_rows = lax.all_gather(key_states, 'blk', axis=0, tiled=True)  104 us
    all_gather x1, waiting for transfers between devices, body(): value_rows = lax.all_gather(value_states, 'blk', axis=0, tiled=True)  101 us
    dynamic_slice x160, local copies, waits for them, and re-layouts, body(): carried, leftover = lax.scan(visit_block, carried, block_stack)  44.4 us
    dot_general x32, matrix products, attend_tile(): jnp.einsum('hqk,khd->hqd', weights.astype(jnp.bfloat16), value_heads, pre...  35.5 us
    while x160, local copies, waits for them, and re-layouts  25.2 us
    dot_general x32, matrix products, attend_tile(): jnp.einsum('qhd,khd->hqk', query_heads, key_heads, preferred_element_type...  20.3 us
    reduce_sum x32, other arithmetic, attend_tile(): new_sum = running_sum * rescale + jnp.sum(weights, axis=2)  18.4 us
  transfers between devices with their start and end apart: 3, of which 3 were waited for; matrix products, arithmetic and copies ran while one was open for 1% of the time, Pallas kernels for 0%

commit v1 on v0

v1 whole, which is shorter than its diff:
```python
import math

import jax
import jax.numpy as jnp
from jax import lax
from jax.experimental import pallas as pl
from jax.experimental.pallas import tpu as pltpu
from jax.sharding import PartitionSpec as P

HD = 128
UNIT = 128
CAP = 512
N_Z = 8
N_TENSOR = 8
N_BLK = 32
ROWS = 2 * CAP
TILE = 256
NEG = -(2.0**100)
EXP_SCALE = math.log2(math.e) / math.sqrt(HD)
MESH = pl.DeviceIdType.MESH
NT = (((1,), (1,)), ((), ()))


def block_of(z, h, c):
    return lax.rem(z, N_Z) * 4 + h * 2 + c


def kernel(
    q_ref, k_ref, v_ref, w_ref, len_ref, ord_ref, out_ref,
    kv, q2, acc, top, bias, ob, og, wb, total,
    loc, par_s, par_r, ring_s, ring_r, sib_s, sib_r, w_s, w_r, o_s, o_r,
):
    b = lax.axis_index("blk")
    t = lax.axis_index("tensor")
    z = b // 4
    h = lax.rem(b // 2, 2)
    c = lax.rem(b, 2)
    other_b = block_of(z, 1 - h, c)
    sibling = {"blk": block_of(z, h, 1 - c), "tensor": t}
    partner = {"blk": other_b, "tensor": t}
    z_up = {"blk": block_of(z + 1, h, c), "tensor": t}
    z_down = {"blk": block_of(z + N_Z - 1, h, c), "tensor": t}
    my_cols = pl.ds(pl.multiple_of(h * HD, HD), HD)
    other_cols = pl.ds(pl.multiple_of((1 - h) * HD, HD), HD)
    my_head = 2 * t + h

    def tensor_at(step):
        return lax.rem(t + step, N_TENSOR)

    def remote(src, dst, send, recv, device):
        return pltpu.make_async_remote_copy(
            src_ref=src, dst_ref=dst, send_sem=send, recv_sem=recv,
            device_id=device, device_id_type=MESH,
        )

    own = [
        pltpu.make_async_copy(k_ref.at[:, my_cols], kv.at[b, 0], loc.at[0]),
        pltpu.make_async_copy(v_ref.at[:, my_cols], kv.at[b, 1], loc.at[1]),
        pltpu.make_async_copy(q_ref.at[:, my_cols], q2.at[pl.ds(0, CAP), pl.ds(0, HD)], loc.at[2]),
        pltpu.make_async_copy(
            w_ref.at[
                pl.ds(pl.multiple_of(c * HD, HD), HD), pl.ds(pl.multiple_of(t * CAP, CAP), CAP)
            ],
            wb.at[2 * t + c],
            loc.at[3],
        ),
    ]
    for copy in own:
        copy.start()

    barrier = pltpu.get_barrier_semaphore()
    peers = [z_up, z_down, sibling]
    peers += [{"blk": b, "tensor": tensor_at(d)} for d in range(1, N_TENSOR)]
    peers += [{"blk": other_b, "tensor": tensor_at(d)} for d in range(N_TENSOR)]
    for peer in peers:
        pl.semaphore_signal(barrier, inc=1, device_id=peer, device_id_type=MESH)

    lane = lax.broadcasted_iota(jnp.int32, (UNIT, 128), 1)
    row = lax.broadcasted_iota(jnp.int32, (UNIT, 128), 0)
    lengths = jnp.broadcast_to(len_ref[...].astype(jnp.float32), (UNIT, 128))
    orders = jnp.broadcast_to(ord_ref[...].astype(jnp.float32), (UNIT, 128))
    holder = lane == row // 4
    unit_start = (lax.rem(row, 4) * UNIT).astype(jnp.float32)
    my_len = jnp.sum(jnp.where(holder, lengths, 0.0), axis=1, keepdims=True)
    my_order = jnp.sum(jnp.where(holder, orders, 0.0), axis=1, keepdims=True)
    before = jnp.where((orders < my_order) & (lane < N_BLK), lengths, 0.0)
    position = jnp.sum(before, axis=1, keepdims=True) + unit_start
    is_live = unit_start < my_len
    query_unit = jnp.where(lane < 4, b * 4 + lane, other_b * 4 + lane - 4)
    chosen = (query_unit == row) & (lane < 8)
    query_position = jnp.sum(jnp.where(chosen, position, 0.0), axis=0, keepdims=True)
    query_live = jnp.sum(jnp.where(chosen & is_live, 1.0, 0.0), axis=0, keepdims=True)
    bias[...] = jnp.where(is_live & (position < query_position), 0.0, NEG)
    tile_row = lax.broadcasted_iota(jnp.int32, (ROWS, HD), 0) // UNIT
    tile_lane = lax.broadcasted_iota(jnp.int32, (ROWS, HD), 1)
    q2[:, HD:] = jnp.where(tile_row == tile_lane, 1.0, 0.0).astype(jnp.bfloat16)

    pl.semaphore_wait(barrier, len(peers))
    for copy in own:
        copy.wait()

    def ring_copy(slot, part, way, step):
        index = part * 8 + way * 4 + step
        device = z_up if way == 0 else z_down
        return remote(kv.at[slot], kv.at[slot], ring_s.at[index], ring_r.at[index], device)

    def sib_copy(slot, index):
        return remote(kv.at[slot], kv.at[slot], sib_s.at[index], sib_r.at[index], sibling)

    ring_copy(b, 0, 0, 0).start()
    ring_copy(b, 0, 1, 0).start()
    swaps = [
        remote(k_ref.at[:, other_cols], kv.at[b, 0], par_s.at[0], par_r.at[0], partner),
        remote(v_ref.at[:, other_cols], kv.at[b, 1], par_s.at[1], par_r.at[1], partner),
        remote(
            q_ref.at[:, other_cols],
            q2.at[pl.ds(CAP, CAP), pl.ds(0, HD)],
            par_s.at[2],
            par_r.at[2],
            partner,
        ),
    ]
    for copy in swaps:
        copy.start()
    sib_copy(b, 0).start()

    square_row = lax.broadcasted_iota(jnp.int32, (UNIT, UNIT), 0)
    square_lane = lax.broadcasted_iota(jnp.int32, (UNIT, UNIT), 1)

    def diagonal(slot, first):
        def unit(i, carry):
            rows = pl.ds(pl.multiple_of((first + i) * UNIT, UNIT), UNIT)
            keys = pl.ds(pl.multiple_of(i * UNIT, UNIT), UNIT)
            k = kv[slot, 0, keys, :]
            v = kv[slot, 1, keys, :]
            s = lax.dot_general(q2[rows, :HD], k, NT, preferred_element_type=jnp.float32)
            s = jnp.where(square_lane <= square_row, s, NEG)
            best = jnp.broadcast_to(jnp.max(s, axis=1, keepdims=True), (UNIT, HD))
            p = jnp.exp2((s - best) * EXP_SCALE).astype(jnp.bfloat16)
            top[rows, :] = best
            acc[rows, :] = jnp.dot(
                p,
                jnp.concatenate([v, jnp.ones_like(v)], axis=1),
                preferred_element_type=jnp.float32,
            )
            return carry

        lax.fori_loop(0, 4, unit, 0)

    diagonal(b, 0)
    remote(kv.at[b, 0], kv.at[other_b, 0], par_s.at[0], par_r.at[0], partner).wait_recv()
    remote(kv.at[b, 1], kv.at[other_b, 1], par_s.at[1], par_r.at[1], partner).wait_recv()
    ring_copy(other_b, 1, 0, 0).start()
    ring_copy(other_b, 1, 1, 0).start()
    sib_copy(other_b, 8).start()
    swaps[2].wait_recv()
    diagonal(other_b, 4)

    def w_copy(step):
        target = tensor_at(step)
        return remote(
            w_ref.at[
                pl.ds(pl.multiple_of(c * HD, HD), HD), pl.ds(pl.multiple_of(target * CAP, CAP), CAP)
            ],
            wb.at[2 * t + c],
            w_s.at[step - 1],
            w_r.at[step - 1],
            {"blk": b, "tensor": target},
        )

    def w_arrived(step):
        source = tensor_at(N_TENSOR - step)
        slot = wb.at[2 * source + c]
        remote(slot, slot, w_s.at[step - 1], w_r.at[step - 1], sibling).wait_recv()

    def w_sib(j):
        slot = wb.at[2 * j + c]
        return remote(slot, slot, w_s.at[7 + j], w_r.at[7 + j], sibling)

    def w_sib_arrived(j):
        slot = wb.at[2 * j + 1 - c]
        remote(slot, slot, w_s.at[7 + j], w_r.at[7 + j], sibling).wait_recv()

    def attend(slot_x, slot_y):
        keys = jnp.concatenate([kv[slot_x, 0], kv[slot_y, 0]], axis=0)
        values = jnp.concatenate([kv[slot_x, 1], kv[slot_y, 1]], axis=0)
        fills = []
        for slot in (slot_x, slot_y):
            for j in range(4):
                fills.append(jnp.broadcast_to(bias[pl.ds(slot * 4 + j, 1), :], (UNIT, HD)))
        keys = jnp.concatenate([keys, jnp.concatenate(fills, axis=0).astype(jnp.bfloat16)], axis=1)
        values = jnp.concatenate([values, jnp.ones_like(values)], axis=1)
        for i in range(ROWS // TILE):
            rows = pl.ds(i * TILE, TILE)
            s = lax.dot_general(q2[rows, :], keys, NT, preferred_element_type=jnp.float32)
            old = top[rows, :]
            best = jnp.maximum(old, jnp.max(s, axis=1, keepdims=True))
            shrink = jnp.exp2((old - best) * EXP_SCALE)
            top[rows, :] = best
            p = jnp.concatenate(
                [
                    jnp.exp2((s[:, j * 128 : (j + 1) * 128] - best) * EXP_SCALE).astype(
                        jnp.bfloat16
                    )
                    for j in range(s.shape[1] // 128)
                ],
                axis=1,
            )
            update = jnp.dot(p, values, preferred_element_type=jnp.float32)
            acc[rows, :] = acc[rows, :] * jnp.concatenate([shrink, shrink], axis=1) + update

    def ring_step(s, part, way):
        side = lax.rem(h + part, 2)
        slot = block_of(z + (N_Z - s if way == 0 else s), side, c)
        ring_copy(slot, part, way, s - 1).wait_recv()
        reach = 4 if part == way else 3

        @pl.when(s < reach)
        def _():
            ring_copy(slot, part, way, s).start()

        sib_copy(slot, part * 8 + (N_Z - s if way == 0 else s)).start()

    def sib_wait(part, distance):
        side = lax.rem(h + part, 2)
        slot = block_of(z + distance, side, 1 - c)
        sib_copy(slot, part * 8 + distance).wait_recv()

    def distance_step(s, carry):
        single = 1 - (lax.rem(s, 4) + 3) // 4

        def phase(ph, inner):
            part = ph // 2
            core = lax.rem(c + ph, 2)

            @pl.when((s > 0) & (s < 4) & (lax.rem(ph, 2) == 0))
            def _():
                ring_step_both(s, part)

            @pl.when((s > 0) & (s < 4) & (lax.rem(ph, 2) == 1))
            def _():
                sib_wait(part, N_Z - s)
                sib_wait(part, s)

            @pl.when((s == 4) & (ph == 0))
            def _():
                ring_step(s, 0, 0)
                ring_step(s, 1, 1)

            @pl.when(((s == 4) | (s == 0)) & (ph == 1))
            def _():
                sib_wait(0, s)
                sib_wait(1, s)

            @pl.when((s == 1) & (ph == 0))
            def _():
                for step in range(1, N_TENSOR):
                    w_copy(step).start()

            @pl.when((s == 3) & (ph == 3))
            def _():
                for step in range(1, N_TENSOR):
                    w_arrived(step)
                for j in range(N_TENSOR):
                    w_sib(j).start()

            side_x = lax.rem(h + part, 2)
            side_y = lax.rem(h + part + single, 2)
            attend(block_of(z + N_Z - s, side_x, core), block_of(z + s, side_y, core))
            return inner

        lax.fori_loop(0, 4 - 2 * single, phase, 0)
        return carry

    def ring_step_both(s, part):
        for p in range(2):

            @pl.when(part == p)
            def _():
                ring_step(s, p, 0)
                ring_step(s, p, 1)

    lax.fori_loop(0, 5, distance_step, 0)

    def finish(half):
        for i in range(4):
            rows = pl.ds(half * CAP + i * UNIT, UNIT)
            unit_live = jnp.sum(
                jnp.where(lane[:1, :] == half * 4 + i, query_live, 0.0), axis=1, keepdims=True
            )
            o = jnp.where(unit_live > 0.0, acc[rows, :HD] / acc[rows, HD:], 0.0)
            ob[half, pl.ds(i * UNIT, UNIT), :] = o.astype(jnp.bfloat16)

    def o_copy(half, step):
        index = half * 7 + step if half else step - 1
        device = {"blk": other_b if half else b, "tensor": tensor_at(step)}
        return remote(ob.at[half], og.at[my_head], o_s.at[index], o_r.at[my_head], device)

    finish(1)
    for step in range(N_TENSOR):
        o_copy(1, step).start()
    finish(0)
    for step in range(1, N_TENSOR):
        o_copy(0, step).start()
    og[my_head] = ob[0]
    for j in range(N_TENSOR):
        w_sib_arrived(j)

    def arrived(head):
        remote(ob.at[0], og.at[head], o_s.at[0], o_r.at[head], partner).wait_recv()

    total[...] = jnp.zeros_like(total)
    for step in range(N_TENSOR):
        j = tensor_at(step)
        if step > 0:
            arrived(2 * j + h)
        arrived(2 * j + 1 - h)
        rows = jnp.concatenate([og[2 * j], og[2 * j + 1]], axis=1)
        weight = jnp.concatenate([wb[2 * j], wb[2 * j + 1]], axis=0)
        total[...] += jnp.dot(rows, weight, preferred_element_type=jnp.float32)
    out_ref[...] = total[...].astype(jnp.bfloat16)

    for copy in swaps:
        copy.wait_send()
    for step in range(1, N_TENSOR):
        w_copy(step).wait_send()
        o_copy(0, step).wait_send()
    for step in range(N_TENSOR):
        w_sib(step).wait_send()
        o_copy(1, step).wait_send()

    def sent(index, carry):
        sib_copy(0, index).wait_send()
        return carry

    lax.fori_loop(0, 16, sent, 0)
    for part in range(2):
        for way in range(2):
            for step in range(4 if part == way else 3):
                ring_copy(0, part, way, step).wait_send()


def body(queries, key_states, value_states, out_weight, lengths, cycle_order):
    pad = lambda a: jnp.pad(a, (0, 128 - N_BLK)).reshape(1, 128)
    any_space = pl.BlockSpec(memory_space=pl.ANY)
    vmem = pl.BlockSpec(memory_space=pltpu.VMEM)
    dma = pltpu.SemaphoreType.DMA
    return pl.pallas_call(
        kernel,
        out_shape=jax.ShapeDtypeStruct((CAP, CAP), jnp.bfloat16),
        in_specs=[any_space] * 4 + [vmem] * 2,
        out_specs=vmem,
        scratch_shapes=[
            pltpu.VMEM((N_BLK, 2, CAP, HD), jnp.bfloat16),
            pltpu.VMEM((ROWS, 2 * HD), jnp.bfloat16),
            pltpu.VMEM((ROWS, 2 * HD), jnp.float32),
            pltpu.VMEM((ROWS, HD), jnp.float32),
            pltpu.VMEM((UNIT, 128), jnp.float32),
            pltpu.VMEM((2, CAP, HD), jnp.bfloat16),
            pltpu.VMEM((2 * N_TENSOR, CAP, HD), jnp.bfloat16),
            pltpu.VMEM((2 * N_TENSOR, HD, CAP), jnp.bfloat16),
            pltpu.VMEM((CAP, CAP), jnp.float32),
            dma((4,)),
            dma((3,)),
            dma((3,)),
            dma((16,)),
            dma((16,)),
            dma((16,)),
            dma((16,)),
            dma((15,)),
            dma((15,)),
            dma((15,)),
            dma((16,)),
        ],
        compiler_params=pltpu.CompilerParams(
            collective_id=0, has_side_effects=True, vmem_limit_bytes=56 * 2**20
        ),
        name="ring_attention",
    )(queries, key_states, value_states, out_weight, pad(lengths), pad(cycle_order))


def solution(mesh):
    placed = (
        P("blk", "tensor"),
        P("blk", "tensor"),
        P("blk", "tensor"),
        P("tensor", None),
        P(),
        P(),
    )
    return jax.shard_map(
        body, mesh=mesh, in_specs=placed, out_specs=P("blk", "tensor"), check_vma=False
    )
```

time: 556 us -> 96.9 us (0.17)
  waiting for transfers between devices: 374 us -> 0 us
  Pallas kernels: 0 us -> 93.7 us
  local copies, waits for them, and re-layouts: 70.8 us -> 3.05 us
  matrix products: 61.5 us -> 0 us
  other arithmetic: 32.5 us -> 0 us
  between operations: 13.2 us -> 0.01 us
    all_gather x2 -> x0, waiting for transfers between devices: 205 us -> none  [the longest x1 104 us: body(): key_rows = lax.all_gather(key_states, 'blk', axis=0, tiled=True)]
    reduce_scatter x1 -> x0, waiting for transfers between devices: 168 us -> none  [body(): lax.psum_scatter(partial_value, 'tensor', scatter_dimension=1, tiled=True)]
    pallas_call x0 -> x1, Pallas kernels: none -> 93.7 us  [body(): pl.pallas_call(kernel, out_shape=jax.ShapeDtypeStruct((CAP, CAP), jnp.bfl...]
    dot_general x65 -> x0, matrix products: 61.5 us -> none  [the longest x32 35.5 us: attend_tile(): jnp.einsum('hqk,khd->hqd', weights.astype(jnp.bfloat16), value_heads, pre...]
    dynamic_slice x160 -> x0, local copies, waits for them, and re-layouts: 44.4 us -> none  [body(): carried, leftover = lax.scan(visit_block, carried, block_stack)]
    while x160 -> x0, local copies, waits for them, and re-layouts: 25.2 us -> none
    reduce_sum x35 -> x0, other arithmetic: 20.8 us -> none  [the longest x32 18.4 us: attend_tile(): new_sum = running_sum * rescale + jnp.sum(weights, axis=2)]
    and x32 -> x0, other arithmetic: 8.69 us -> none  [attend_tile(): query_valid[:, None] & key_valid[None, :]]
  transfers between devices with their start and end apart: 3 -> 0, of which waited for: 3 -> 0; matrix products, arithmetic and copies ran while one was open for 1% -> 0% of each run, Pallas kernels for 0% -> 0%
where the time goes in v1:
time: 96.9 us; the launch traced here: 96.8 us
  Pallas kernels  93.7 us (97%)
  local copies, waits for them, and re-layouts  3.05 us (3%)
    pallas_call x1, Pallas kernels, body(): pl.pallas_call(kernel, out_shape=jax.ShapeDtypeStruct((CAP, CAP), jnp.bfl...  93.7 us

profile of v1, /device:TPU:1, one launch (start us, length us, event | category | flops | bytes accessed | tf_op | source)
XLA Modules:
  0.0 96.8 jit_solution(593154627038256402)
XLA Ops:
  0.0 1.2 %pad_bitcast_fusion = (s32[1,128]{1,0:T(1,128)}, s32[1,128]{1,0:T(1,128)}) fusion(s32[32]{0:T(128)} %param.11, s32[32]{0:T(128)} %param.10), kind=kLoop, calls=%fused_computation | loop fusion | bytes 1280 | tf_op jit(solution)/shard_map/reshape | solution.py:344
  1.2 93.7 %ring_attention.1 = bf16[512,512]{1,0:T(8,128)(2,1)} custom-call(bf16[512,256]{1,0:T(8,128)(2,1)} %q_ref.1, bf16[512,256]{1,0:T(8,128)(2,1)} %k_ref.1, bf16[512,256]{1,0:T(8,128)(2,1)} %v_ref.1, bf16[256,4096]{1,0:T(8,128)(2,1)} %w_ref.1, s32[1,128]{1,0:T(1,128)} %get-tuple-element.6.len_ref, s32[1,128]{1,0:T(1,128)} %get-tuple-element.5.ord_ref), custom_call_target="tpu_custom_call" | custom-call | tf_op jit(solution)/shard_map/ring_attention/pallas_call | solution.py:348
  94.9 1.9 %copy.8 = bf16[512,512]{1,0:T(8,128)(2,1)} copy(bf16[512,512]{1,0:T(8,128)(2,1)} %ring_attention.1) | data formatting | bytes 1048576

commit v2 on v1

--- a/solution.py
+++ b/solution.py
@@ -1,3 +1,4 @@
+import functools
 import math
 
 import jax
@@ -27,14 +28,16 @@
 
 def kernel(
     q_ref, k_ref, v_ref, w_ref, len_ref, ord_ref, out_ref,
-    kv, q2, acc, top, bias, ob, og, wb, total,
-    loc, par_s, par_r, ring_s, ring_r, sib_s, sib_r, w_s, w_r, o_s, o_r,
+    kv, q2, acc, top, bias, ob, og, wb, total, transit,
+    loc, par_s, par_r, ring_s, ring_r, sib_s, sib_r, w_s, w_r, o_s, o_r, t_r,
 ):
     b = lax.axis_index("blk")
     t = lax.axis_index("tensor")
     z = b // 4
     h = lax.rem(b // 2, 2)
     c = lax.rem(b, 2)
+    y = t // 2
+    x_lo = lax.rem(t, 2)
     other_b = block_of(z, 1 - h, c)
     sibling = {"blk": block_of(z, h, 1 - c), "tensor": t}
     partner = {"blk": other_b, "tensor": t}
@@ -71,19 +74,19 @@
     barrier = pltpu.get_barrier_semaphore()
     peers = [z_up, z_down, sibling]
     peers += [{"blk": b, "tensor": tensor_at(d)} for d in range(1, N_TENSOR)]
-    peers += [{"blk": other_b, "tensor": tensor_at(d)} for d in range(N_TENSOR)]
+    peers += [{"blk": other_b, "tensor": 2 * y + side} for side in range(2)]
     for peer in peers:
         pl.semaphore_signal(barrier, inc=1, device_id=peer, device_id_type=MESH)
 
     lane = lax.broadcasted_iota(jnp.int32, (UNIT, 128), 1)
     row = lax.broadcasted_iota(jnp.int32, (UNIT, 128), 0)
-    lengths = jnp.broadcast_to(len_ref[...].astype(jnp.float32), (UNIT, 128))
-    orders = jnp.broadcast_to(ord_ref[...].astype(jnp.float32), (UNIT, 128))
-    holder = lane == row // 4
-    unit_start = (lax.rem(row, 4) * UNIT).astype(jnp.float32)
+    lengths = jnp.broadcast_to(len_ref[...].astype(jnp.float32), (UNIT, N_BLK))
+    orders = jnp.broadcast_to(ord_ref[...].astype(jnp.float32), (UNIT, N_BLK))
+    holder = lane[:, :N_BLK] == row[:, :N_BLK] // 4
+    unit_start = (lax.rem(row[:, :1], 4) * UNIT).astype(jnp.float32)
     my_len = jnp.sum(jnp.where(holder, lengths, 0.0), axis=1, keepdims=True)
     my_order = jnp.sum(jnp.where(holder, orders, 0.0), axis=1, keepdims=True)
-    before = jnp.where((orders < my_order) & (lane < N_BLK), lengths, 0.0)
+    before = jnp.where(orders < my_order, lengths, 0.0)
     position = jnp.sum(before, axis=1, keepdims=True) + unit_start
     is_live = unit_start < my_len
     query_unit = jnp.where(lane < 4, b * 4 + lane, other_b * 4 + lane - 4)
@@ -120,8 +123,8 @@
             partner,
         ),
     ]
-    for copy in swaps:
-        copy.start()
+    swaps[0].start()
+    swaps[1].start()
     sib_copy(b, 0).start()
 
     square_row = lax.broadcasted_iota(jnp.int32, (UNIT, UNIT), 0)
@@ -148,6 +151,7 @@
         lax.fori_loop(0, 4, unit, 0)
 
     diagonal(b, 0)
+    swaps[2].start()
     remote(kv.at[b, 0], kv.at[other_b, 0], par_s.at[0], par_r.at[0], partner).wait_recv()
     remote(kv.at[b, 1], kv.at[other_b, 1], par_s.at[1], par_r.at[1], partner).wait_recv()
     ring_copy(other_b, 1, 0, 0).start()
@@ -291,43 +295,104 @@
             o = jnp.where(unit_live > 0.0, acc[rows, :HD] / acc[rows, HD:], 0.0)
             ob[half, pl.ds(i * UNIT, UNIT), :] = o.astype(jnp.bfloat16)
 
-    def o_copy(half, step):
-        index = half * 7 + step if half else step - 1
-        device = {"blk": other_b if half else b, "tensor": tensor_at(step)}
-        return remote(ob.at[half], og.at[my_head], o_s.at[index], o_r.at[my_head], device)
+    def plane(dy, e_hi, e_lo):
+        side = lax.rem(h + e_hi, 2)
+        column = lax.rem(x_lo + e_lo, 2)
+        return {"blk": block_of(z, side, c), "tensor": 2 * lax.rem(y + dy, 4) + column}
+
+    def head_at(dy, e_hi, e_lo):
+        return (
+            4 * lax.rem(y + dy, 4) + 2 * lax.rem(x_lo + e_lo, 2) + lax.rem(h + e_hi, 2)
+        )
+
+    def send_head(src, dy, e_hi, e_lo, head, index):
+        return remote(src, og.at[head], o_s.at[index], o_r.at[head], plane(dy, e_hi, e_lo))
+
+    def send_transit(dy, index):
+        return remote(ob.at[1], transit.at[dy - 1], o_s.at[index], t_r.at[dy - 1], plane(dy, 0, 0))
+
+    def arrived(head):
+        remote(ob.at[0], og.at[head], o_s.at[0], o_r.at[head], partner).wait_recv()
+
+    def transit_arrived(dy):
+        slot = transit.at[dy - 1]
+        remote(slot, slot, o_s.at[0], t_r.at[dy - 1], partner).wait_recv()
+
+    others = ((1, 0), (1, 1), (0, 1))
+    steps = (1, 3, 2)
 
     finish(1)
-    for step in range(N_TENSOR):
-        o_copy(1, step).start()
+
+    @pl.when(c == 0)
+    def _():
+        send_head(ob.at[1], 0, 1, 0, my_head, 0).start()
+        send_head(ob.at[1], 0, 1, 1, my_head, 1).start()
+
+    @pl.when(c == 1)
+    def _():
+        for i, dy in enumerate(steps):
+            send_transit(dy, i).start()
+
     finish(0)
-    for step in range(1, N_TENSOR):
-        o_copy(0, step).start()
+
+    @pl.when(c == 0)
+    def _():
+        send_head(ob.at[0], 0, 0, 1, my_head, 2).start()
+        for i, dy in enumerate(steps):
+            send_head(ob.at[0], dy, 0, 0, my_head, 3 + i).start()
+        for k, (e_hi, e_lo) in enumerate(((0, 1), (1, 0), (1, 1))):
+            head = head_at(0, e_hi, e_lo)
+            arrived(head)
+            for i, dy in enumerate(steps):
+                send_head(og.at[head], dy, 0, 0, head, 6 + 3 * k + i).start()
+
+    @pl.when(c == 1)
+    def _():
+        for i, dy in enumerate(steps):
+            send_head(ob.at[0], dy, 0, 0, my_head, 3 + i).start()
+        for i, (e_hi, e_lo) in enumerate(others):
+            send_head(ob.at[e_hi], 0, e_hi, e_lo, my_head, 6 + i).start()
+        for k, dy in enumerate(steps):
+            transit_arrived(dy)
+            head = head_at(4 - dy, 0, 0)
+            send_head(transit.at[dy - 1], 0, 1, 0, head, 9 + 3 * k).start()
+            send_head(transit.at[dy - 1], 0, 1, 1, head, 10 + 3 * k).start()
+            arrived(head)
+            send_head(og.at[head], 0, 0, 1, head, 11 + 3 * k).start()
+
     og[my_head] = ob[0]
     for j in range(N_TENSOR):
         w_sib_arrived(j)
 
-    def arrived(head):
-        remote(ob.at[0], og.at[head], o_s.at[0], o_r.at[head], partner).wait_recv()
-
     total[...] = jnp.zeros_like(total)
-    for step in range(N_TENSOR):
-        j = tensor_at(step)
-        if step > 0:
-            arrived(2 * j + h)
-        arrived(2 * j + 1 - h)
-        rows = jnp.concatenate([og[2 * j], og[2 * j + 1]], axis=1)
-        weight = jnp.concatenate([wb[2 * j], wb[2 * j + 1]], axis=0)
-        total[...] += jnp.dot(rows, weight, preferred_element_type=jnp.float32)
+    for dy in (0, 1, 3, 2):
+        for e_lo in range(2):
+            first = 4 * lax.rem(y + dy, 4) + 2 * lax.rem(x_lo + e_lo, 2)
+
+            for e_hi in range(2):
+                head = head_at(dy, e_hi, e_lo)
+                if dy > 0:
+                    pl.when(c == 0)(functools.partial(arrived, head))
+                if (e_hi, e_lo) != (0, 0):
+                    pl.when(c == 1)(functools.partial(arrived, head))
+            rows = jnp.concatenate([og[first], og[first + 1]], axis=1)
+            weight = jnp.concatenate([wb[first], wb[first + 1]], axis=0)
+            total[...] += jnp.dot(rows, weight, preferred_element_type=jnp.float32)
     out_ref[...] = total[...].astype(jnp.bfloat16)
 
     for copy in swaps:
         copy.wait_send()
     for step in range(1, N_TENSOR):
         w_copy(step).wait_send()
-        o_copy(0, step).wait_send()
     for step in range(N_TENSOR):
         w_sib(step).wait_send()
-        o_copy(1, step).wait_send()
+    for index in range(15):
+        send_head(ob.at[0], 1, 0, 0, my_head, index).wait_send()
+
+    @pl.when(c == 1)
+    def _():
+        for index in range(15, 18):
+            send_head(ob.at[0], 1, 0, 0, my_head, index).wait_send()
 
     def sent(index, carry):
         sib_copy(0, index).wait_send()
@@ -341,7 +406,6 @@
 
 
 def body(queries, key_states, value_states, out_weight, lengths, cycle_order):
-    pad = lambda a: jnp.pad(a, (0, 128 - N_BLK)).reshape(1, 128)
     any_space = pl.BlockSpec(memory_space=pl.ANY)
     vmem = pl.BlockSpec(memory_space=pltpu.VMEM)
     dma = pltpu.SemaphoreType.DMA
@@ -360,6 +424,7 @@
             pltpu.VMEM((2 * N_TENSOR, CAP, HD), jnp.bfloat16),
             pltpu.VMEM((2 * N_TENSOR, HD, CAP), jnp.bfloat16),
             pltpu.VMEM((CAP, CAP), jnp.float32),
+            pltpu.VMEM((3, CAP, HD), jnp.bfloat16),
             dma((4,)),
             dma((3,)),
             dma((3,)),
@@ -369,14 +434,15 @@
             dma((16,)),
             dma((15,)),
             dma((15,)),
-            dma((15,)),
+            dma((18,)),
             dma((16,)),
+            dma((3,)),
         ],
         compiler_params=pltpu.CompilerParams(
             collective_id=0, has_side_effects=True, vmem_limit_bytes=56 * 2**20
         ),
         name="ring_attention",
-    )(queries, key_states, value_states, out_weight, pad(lengths), pad(cycle_order))
+    )(queries, key_states, value_states, out_weight, lengths.reshape(1, N_BLK), cycle_order.reshape(1, N_BLK))
 
 
 def solution(mesh):

time: 96.9 us -> 83.2 us (0.86)
  Pallas kernels: 93.7 us -> 80.4 us
  local copies, waits for them, and re-layouts: 3.05 us -> 1.87 us
    pallas_call x1, Pallas kernels: 93.7 us -> 80.4 us  [body(): pl.pallas_call(kernel, out_shape=jax.ShapeDtypeStruct((CAP, CAP), jnp.bfl...]
    reshape x1 -> x0, local copies, waits for them, and re-layouts: 1.19 us -> none  [body(): pad = lambda a: jnp.pad(a, (0, 128 - N_BLK)).reshape(1, 128)]
where the time goes in v2:
time: 83.2 us; the launch traced here: 82.3 us
  Pallas kernels  80.4 us (97%)
  local copies, waits for them, and re-layouts  1.87 us (2%)
    pallas_call x1, Pallas kernels, body(): pl.pallas_call(kernel, out_shape=jax.ShapeDtypeStruct((CAP, CAP), jnp.bfl...  80.4 us
    unnamed x1, local copies, waits for them, and re-layouts  1.87 us

profile of v2, /device:TPU:1, one launch (start us, length us, event | category | flops | bytes accessed | tf_op | source)
XLA Modules:
  0.0 82.3 jit_solution(4986304058793410036)
XLA Ops:
  0.0 80.4 %ring_attention.1 = bf16[512,512]{1,0:T(8,128)(2,1)} custom-call(bf16[512,256]{1,0:T(8,128)(2,1)} %q_ref.1, bf16[512,256]{1,0:T(8,128)(2,1)} %k_ref.1, bf16[512,256]{1,0:T(8,128)(2,1)} %v_ref.1, bf16[256,4096]{1,0:T(8,128)(2,1)} %w_ref.1, s32[1,32]{1,0:T(1,128)} %bitcast.2, s32[1,32]{1,0:T(1,128)} %bitcast.3), custom_call_target="tpu_custom_call" | custom-call | tf_op jit(solution)/shard_map/ring_attention/pallas_call | solution.py:412
  80.4 1.9 %copy.8 = bf16[512,512]{1,0:T(8,128)(2,1)} copy(bf16[512,512]{1,0:T(8,128)(2,1)} %ring_attention.1) | data formatting | bytes 1048576

commit v3 on v2

--- a/solution.py
+++ b/solution.py
@@ -16,7 +16,9 @@
 N_BLK = 32
 ROWS = 2 * CAP
 TILE = 256
+HALF = CAP // 2
 NEG = -(2.0**100)
+LOWEST = -(2.0**99)
 EXP_SCALE = math.log2(math.e) / math.sqrt(HD)
 MESH = pl.DeviceIdType.MESH
 NT = (((1,), (1,)), ((), ()))
@@ -29,7 +31,7 @@
 def kernel(
     q_ref, k_ref, v_ref, w_ref, len_ref, ord_ref, out_ref,
     kv, q2, acc, top, bias, ob, og, wb, total, transit,
-    loc, par_s, par_r, ring_s, ring_r, sib_s, sib_r, w_s, w_r, o_s, o_r, t_r,
+    loc, par_s, par_r, ring_s, ring_r, sib_s, sib_r, w_s, w_r, o_s, o_r, t_r, hs_s, h_r,
 ):
     b = lax.axis_index("blk")
     t = lax.axis_index("tensor")
@@ -102,30 +104,88 @@
     for copy in own:
         copy.wait()
 
-    def ring_copy(slot, part, way, step):
-        index = part * 8 + way * 4 + step
+    def piece(slot, half):
+        return kv.at[slot, :, pl.ds(pl.multiple_of(half * HALF, HALF), HALF), :]
+
+    def ring_copy(slot, part, half, way, step):
+        index = part * 16 + half * 8 + way * 4 + step
         device = z_up if way == 0 else z_down
-        return remote(kv.at[slot], kv.at[slot], ring_s.at[index], ring_r.at[index], device)
-
-    def sib_copy(slot, index):
-        return remote(kv.at[slot], kv.at[slot], sib_s.at[index], sib_r.at[index], sibling)
-
-    ring_copy(b, 0, 0, 0).start()
-    ring_copy(b, 0, 1, 0).start()
-    swaps = [
-        remote(k_ref.at[:, other_cols], kv.at[b, 0], par_s.at[0], par_r.at[0], partner),
-        remote(v_ref.at[:, other_cols], kv.at[b, 1], par_s.at[1], par_r.at[1], partner),
-        remote(
-            q_ref.at[:, other_cols],
-            q2.at[pl.ds(CAP, CAP), pl.ds(0, HD)],
-            par_s.at[2],
-            par_r.at[2],
+        at = piece(slot, half)
+        return remote(at, at, ring_s.at[index], ring_r.at[index], device)
+
+    def sib_copy(slot, part, half, distance):
+        index = part * 16 + half * 8 + distance
+        at = piece(slot, half)
+        return remote(at, at, sib_s.at[index], sib_r.at[index], sibling)
+
+    def swap(half, which):
+        rows = pl.ds(half * HALF, HALF)
+        index = half * 2 + which
+        source = v_ref if which else k_ref
+        return remote(
+            source.at[rows, other_cols],
+            kv.at[b, which, rows, :],
+            par_s.at[index],
+            par_r.at[index],
             partner,
-        ),
-    ]
-    swaps[0].start()
-    swaps[1].start()
-    sib_copy(b, 0).start()
+        )
+
+    def swapped(half, which):
+        at = kv.at[other_b, which, pl.ds(half * HALF, HALF), :]
+        index = half * 2 + which
+        remote(at, at, par_s.at[index], par_r.at[index], partner).wait_recv()
+
+    swap_q = remote(
+        q_ref.at[:, other_cols],
+        q2.at[pl.ds(CAP, CAP), pl.ds(0, HD)],
+        par_s.at[4],
+        par_r.at[4],
+        partner,
+    )
+
+    def send_own(half):
+        for way in range(2):
+            ring_copy(b, 0, half, way, 0).start()
+        for which in range(2):
+            swap(half, which).start()
+        sib_copy(b, 0, half, 0).start()
+
+    def send_swapped(half):
+        for which in range(2):
+            swapped(half, which)
+        for way in range(2):
+            ring_copy(other_b, 1, half, way, 0).start()
+        sib_copy(other_b, 1, half, 0).start()
+
+    def ring_step(part, hop, half, way, onward):
+        side = lax.rem(h + part, 2)
+        distance = N_Z - hop if way == 0 else hop
+        slot = block_of(z + distance, side, c)
+        ring_copy(slot, part, half, way, hop - 1).wait_recv()
+        if onward is not None:
+
+            @pl.when(onward)
+            def _():
+                ring_copy(slot, part, half, way, hop).start()
+
+        sib_copy(slot, part, half, distance).start()
+
+    def event(part, hop, half):
+        ring_step(part, hop, half, 0, hop < 3)
+        ring_step(part, hop, half, 1, hop < 3 + part)
+
+    def send_fourth():
+        for half in range(2):
+            ring_copy(block_of(z + N_Z - 3, h, c), 0, half, 0, 3).start()
+
+    def last_event(half):
+        ring_step(0, 4, half, 0, None)
+        ring_step(1, 4, half, 1, None)
+
+    swap_q.start()
+    send_own(0)
+    top[...] = jnp.full_like(top, LOWEST)
+    acc[...] = jnp.zeros_like(acc)
 
     square_row = lax.broadcasted_iota(jnp.int32, (UNIT, UNIT), 0)
     square_lane = lax.broadcasted_iota(jnp.int32, (UNIT, UNIT), 1)
@@ -138,10 +198,12 @@
             v = kv[slot, 1, keys, :]
             s = lax.dot_general(q2[rows, :HD], k, NT, preferred_element_type=jnp.float32)
             s = jnp.where(square_lane <= square_row, s, NEG)
-            best = jnp.broadcast_to(jnp.max(s, axis=1, keepdims=True), (UNIT, HD))
+            old = top[rows, :]
+            best = jnp.maximum(old, jnp.max(s, axis=1, keepdims=True))
+            shrink = jnp.exp2((old - best) * EXP_SCALE)
             p = jnp.exp2((s - best) * EXP_SCALE).astype(jnp.bfloat16)
             top[rows, :] = best
-            acc[rows, :] = jnp.dot(
+            acc[rows, :] = acc[rows, :] * jnp.concatenate([shrink, shrink], axis=1) + jnp.dot(
                 p,
                 jnp.concatenate([v, jnp.ones_like(v)], axis=1),
                 preferred_element_type=jnp.float32,
@@ -151,14 +213,9 @@
         lax.fori_loop(0, 4, unit, 0)
 
     diagonal(b, 0)
-    swaps[2].start()
-    remote(kv.at[b, 0], kv.at[other_b, 0], par_s.at[0], par_r.at[0], partner).wait_recv()
-    remote(kv.at[b, 1], kv.at[other_b, 1], par_s.at[1], par_r.at[1], partner).wait_recv()
-    ring_copy(other_b, 1, 0, 0).start()
-    ring_copy(other_b, 1, 1, 0).start()
-    sib_copy(other_b, 8).start()
-    swaps[2].wait_recv()
-    diagonal(other_b, 4)
+    send_own(1)
+    swap_q.wait_recv()
+    event(0, 1, 0)
 
     def w_copy(step):
         target = tensor_at(step)
@@ -185,13 +242,16 @@
         slot = wb.at[2 * j + 1 - c]
         remote(slot, slot, w_s.at[7 + j], w_r.at[7 + j], sibling).wait_recv()
 
-    def attend(slot_x, slot_y):
-        keys = jnp.concatenate([kv[slot_x, 0], kv[slot_y, 0]], axis=0)
-        values = jnp.concatenate([kv[slot_x, 1], kv[slot_y, 1]], axis=0)
+    def attend(slot_x, slot_y, half=None):
+        start, count = (0, CAP) if half is None else (pl.multiple_of(half * HALF, HALF), HALF)
+        rows = pl.ds(start, count)
+        keys = jnp.concatenate([kv[slot_x, 0, rows, :], kv[slot_y, 0, rows, :]], axis=0)
+        values = jnp.concatenate([kv[slot_x, 1, rows, :], kv[slot_y, 1, rows, :]], axis=0)
         fills = []
         for slot in (slot_x, slot_y):
-            for j in range(4):
-                fills.append(jnp.broadcast_to(bias[pl.ds(slot * 4 + j, 1), :], (UNIT, HD)))
+            first = slot * 4 if half is None else slot * 4 + half * 2
+            for j in range(count // UNIT):
+                fills.append(jnp.broadcast_to(bias[pl.ds(first + j, 1), :], (UNIT, HD)))
         keys = jnp.concatenate([keys, jnp.concatenate(fills, axis=0).astype(jnp.bfloat16)], axis=1)
         values = jnp.concatenate([values, jnp.ones_like(values)], axis=1)
         for i in range(ROWS // TILE):
@@ -213,78 +273,99 @@
             update = jnp.dot(p, values, preferred_element_type=jnp.float32)
             acc[rows, :] = acc[rows, :] * jnp.concatenate([shrink, shrink], axis=1) + update
 
-    def ring_step(s, part, way):
-        side = lax.rem(h + part, 2)
-        slot = block_of(z + (N_Z - s if way == 0 else s), side, c)
-        ring_copy(slot, part, way, s - 1).wait_recv()
-        reach = 4 if part == way else 3
-
-        @pl.when(s < reach)
-        def _():
-            ring_copy(slot, part, way, s).start()
-
-        sib_copy(slot, part * 8 + (N_Z - s if way == 0 else s)).start()
-
-    def sib_wait(part, distance):
+    def sib_wait(part, half, distance):
         side = lax.rem(h + part, 2)
         slot = block_of(z + distance, side, 1 - c)
-        sib_copy(slot, part * 8 + distance).wait_recv()
-
-    def distance_step(s, carry):
-        single = 1 - (lax.rem(s, 4) + 3) // 4
+        sib_copy(slot, part, half, distance).wait_recv()
+
+    for half in range(2):
+        sib_wait(0, half, 0)
+    attend(b, block_of(z, h, 1 - c))
+
+    def round_step(r, carry):
+        part = 1 - lax.rem(r, 2)
+        s = (r + 1) // 2 - part
+        single = (4 - s) // 4
 
         def phase(ph, inner):
-            part = ph // 2
             core = lax.rem(c + ph, 2)
 
-            @pl.when((s > 0) & (s < 4) & (lax.rem(ph, 2) == 0))
-            def _():
-                ring_step_both(s, part)
-
-            @pl.when((s > 0) & (s < 4) & (lax.rem(ph, 2) == 1))
-            def _():
-                sib_wait(part, N_Z - s)
-                sib_wait(part, s)
-
-            @pl.when((s == 4) & (ph == 0))
-            def _():
-                ring_step(s, 0, 0)
-                ring_step(s, 1, 1)
-
-            @pl.when(((s == 4) | (s == 0)) & (ph == 1))
-            def _():
-                sib_wait(0, s)
-                sib_wait(1, s)
-
-            @pl.when((s == 1) & (ph == 0))
-            def _():
+            @pl.when((ph == 0) & ((r == 1) | (r > 3)))
+            def _():
+                event(part, s, 1)
+
+            @pl.when((ph == 0) & (r == 1))
+            def _():
+                send_swapped(0)
+
+            @pl.when((ph == 1) & (r == 1))
+            def _():
+                send_swapped(1)
+                event(0, 2, 0)
+
+            @pl.when(r == 2)
+            def _():
+                event(0, 2, 1)
                 for step in range(1, N_TENSOR):
                     w_copy(step).start()
-
-            @pl.when((s == 3) & (ph == 3))
-            def _():
+                diagonal(other_b, 4)
+                for half in range(2):
+                    sib_wait(1, half, 0)
+
+            @pl.when((ph == 0) & (r == 6))
+            def _():
+                send_fourth()
+
+            @pl.when((ph == 1) & (r > 2) & (r < 6))
+            def _():
+                following = 1 - part
+                event(following, (r + 2) // 2 - following, 0)
+
+            @pl.when((ph == 1) & (r == 6))
+            def _():
+                event(1, 3, 0)
                 for step in range(1, N_TENSOR):
                     w_arrived(step)
                 for j in range(N_TENSOR):
                     w_sib(j).start()
 
-            side_x = lax.rem(h + part, 2)
-            side_y = lax.rem(h + part + single, 2)
-            attend(block_of(z + N_Z - s, side_x, core), block_of(z + s, side_y, core))
+            @pl.when((ph == 1) & (r == 8))
+            def _():
+                last_event(0)
+
+            @pl.when(ph == 1)
+            def _():
+                for half in range(2):
+                    sib_wait(part, half, N_Z - s)
+                    sib_wait(part, half, s)
+
+            side = lax.rem(h + part, 2)
+            core_y = lax.rem(core + single, 2)
+            attend(block_of(z + N_Z - s, side, core), block_of(z + s, side, core_y))
             return inner
 
-        lax.fori_loop(0, 4 - 2 * single, phase, 0)
+        lax.fori_loop(0, 2 - single - 2 * (s // 4), phase, 0)
         return carry
 
-    def ring_step_both(s, part):
-        for p in range(2):
-
-            @pl.when(part == p)
-            def _():
-                ring_step(s, p, 0)
-                ring_step(s, p, 1)
-
-    lax.fori_loop(0, 5, distance_step, 0)
+    lax.fori_loop(1, 9, round_step, 0)
+
+    def last_step(i, carry):
+        half = i // 2
+        core = lax.rem(c + i, 2)
+
+        @pl.when(i == 2)
+        def _():
+            last_event(1)
+
+        @pl.when(lax.rem(i, 2) == 1)
+        def _():
+            sib_wait(0, half, 4)
+            sib_wait(1, half, 4)
+
+        attend(block_of(z + 4, h, core), block_of(z + 4, 1 - h, core), half)
+        return carry
+
+    lax.fori_loop(0, 4, last_step, 0)
 
     def finish(half):
         for i in range(4):
@@ -318,6 +399,14 @@
         slot = transit.at[dy - 1]
         remote(slot, slot, o_s.at[0], t_r.at[dy - 1], partner).wait_recv()
 
+    def send_half(half, dy, head, index):
+        at = og.at[head, pl.ds(half * HALF, HALF), :]
+        return remote(at, at, hs_s.at[index], h_r.at[half * 16 + head], plane(dy, 0, 0))
+
+    def half_arrived(half, head):
+        at = og.at[head, pl.ds(half * HALF, HALF), :]
+        remote(at, at, hs_s.at[0], h_r.at[half * 16 + head], partner).wait_recv()
+
     others = ((1, 0), (1, 1), (0, 1))
     steps = (1, 3, 2)
 
@@ -338,13 +427,20 @@
     @pl.when(c == 0)
     def _():
         send_head(ob.at[0], 0, 0, 1, my_head, 2).start()
-        for i, dy in enumerate(steps):
+        for i, dy in enumerate((1, 3)):
             send_head(ob.at[0], dy, 0, 0, my_head, 3 + i).start()
-        for k, (e_hi, e_lo) in enumerate(((0, 1), (1, 0), (1, 1))):
-            head = head_at(0, e_hi, e_lo)
-            arrived(head)
-            for i, dy in enumerate(steps):
-                send_head(og.at[head], dy, 0, 0, head, 6 + 3 * k + i).start()
+        lanes = ((0, 0), (0, 1), (1, 1), (1, 0))
+        for k, (e_hi, e_lo) in enumerate(lanes):
+            if k > 0:
+                head = head_at(0, e_hi, e_lo)
+                arrived(head)
+                for i, dy in enumerate((1, 3)):
+                    send_head(og.at[head], dy, 0, 0, head, 3 + 2 * k + i).start()
+        for k, (e_hi, e_lo) in enumerate(lanes):
+            for i, dy in enumerate((1, 3)):
+                head = head_at(4 - dy, e_hi, e_lo)
+                arrived(head)
+                send_half(i, dy, head, 2 * k + i).start()
 
     @pl.when(c == 1)
     def _():
@@ -371,8 +467,9 @@
 
             for e_hi in range(2):
                 head = head_at(dy, e_hi, e_lo)
-                if dy > 0:
-                    pl.when(c == 0)(functools.partial(arrived, head))
+                if dy == 2:
+                    pl.when(c == 0)(functools.partial(half_arrived, 0, head))
+                    pl.when(c == 0)(functools.partial(half_arrived, 1, head))
                 if (e_hi, e_lo) != (0, 0):
                     pl.when(c == 1)(functools.partial(arrived, head))
             rows = jnp.concatenate([og[first], og[first + 1]], axis=1)
@@ -380,29 +477,46 @@
             total[...] += jnp.dot(rows, weight, preferred_element_type=jnp.float32)
     out_ref[...] = total[...].astype(jnp.bfloat16)
 
-    for copy in swaps:
-        copy.wait_send()
+    for half in range(2):
+        for which in range(2):
+            swap(half, which).wait_send()
+    swap_q.wait_send()
     for step in range(1, N_TENSOR):
         w_copy(step).wait_send()
     for step in range(N_TENSOR):
         w_sib(step).wait_send()
-    for index in range(15):
+
+    def head_sent(index, carry):
         send_head(ob.at[0], 1, 0, 0, my_head, index).wait_send()
-
-    @pl.when(c == 1)
-    def _():
-        for index in range(15, 18):
-            send_head(ob.at[0], 1, 0, 0, my_head, index).wait_send()
-
-    def sent(index, carry):
-        sib_copy(0, index).wait_send()
         return carry
 
-    lax.fori_loop(0, 16, sent, 0)
-    for part in range(2):
+    def relay_sent(index, carry):
+        send_half(0, 1, my_head, index).wait_send()
+        return carry
+
+    lax.fori_loop(0, 11 + 7 * c, head_sent, 0)
+    lax.fori_loop(0, 8 * (1 - c), relay_sent, 0)
+
+    def sent(i, carry):
+        part = i // 2
+        half = lax.rem(i, 2)
+
+        def sib_sent(distance, inner):
+            sib_copy(0, part, half, distance).wait_send()
+            return inner
+
+        lax.fori_loop(0, N_Z, sib_sent, 0)
         for way in range(2):
-            for step in range(4 if part == way else 3):
-                ring_copy(0, part, way, step).wait_send()
+
+            def ring_sent(step, inner, way=way):
+                ring_copy(0, part, half, way, step).wait_send()
+                return inner
+
+            reach = 4 - part if way == 0 else 3 + part
+            lax.fori_loop(0, reach, ring_sent, 0)
+        return carry
+
+    lax.fori_loop(0, 4, sent, 0)
 
 
 def body(queries, key_states, value_states, out_weight, lengths, cycle_order):
@@ -426,17 +540,19 @@
             pltpu.VMEM((CAP, CAP), jnp.float32),
             pltpu.VMEM((3, CAP, HD), jnp.bfloat16),
             dma((4,)),
-            dma((3,)),
-            dma((3,)),
-            dma((16,)),
-            dma((16,)),
-            dma((16,)),
-            dma((16,)),
+            dma((5,)),
+            dma((5,)),
+            dma((32,)),
+            dma((32,)),
+            dma((32,)),
+            dma((32,)),
             dma((15,)),
             dma((15,)),
             dma((18,)),
             dma((16,)),
             dma((3,)),
+            dma((8,)),
+            dma((32,)),
         ],
         compiler_params=pltpu.CompilerParams(
             collective_id=0, has_side_effects=True, vmem_limit_bytes=56 * 2**20

time: 83.2 us -> 79.4 us (0.954)
  Pallas kernels: 80.4 us -> 77.4 us
    pallas_call x1, Pallas kernels: 80.4 us -> 77.4 us  [body(): pl.pallas_call(kernel, out_shape=jax.ShapeDtypeStruct((CAP, CAP), jnp.bfl...]
where the time goes in v3:
time: 79.4 us; the launch traced here: 79.2 us
  Pallas kernels  77.4 us (97%)
  local copies, waits for them, and re-layouts  1.87 us (2%)
    pallas_call x1, Pallas kernels, body(): pl.pallas_call(kernel, out_shape=jax.ShapeDtypeStruct((CAP, CAP), jnp.bfl...  77.4 us
    unnamed x1, local copies, waits for them, and re-layouts  1.87 us

profile of v3, /device:TPU:1, one launch (start us, length us, event | category | flops | bytes accessed | tf_op | source)
XLA Modules:
  0.0 79.2 jit_solution(11454727119775543243)
XLA Ops:
  0.0 77.4 %ring_attention.1 = bf16[512,512]{1,0:T(8,128)(2,1)} custom-call(bf16[512,256]{1,0:T(8,128)(2,1)} %q_ref.1, bf16[512,256]{1,0:T(8,128)(2,1)} %k_ref.1, bf16[512,256]{1,0:T(8,128)(2,1)} %v_ref.1, bf16[256,4096]{1,0:T(8,128)(2,1)} %w_ref.1, s32[1,32]{1,0:T(1,128)} %bitcast.2, s32[1,32]{1,0:T(1,128)} %bitcast.3), custom_call_target="tpu_custom_call" | custom-call | tf_op jit(solution)/shard_map/ring_attention/pallas_call | solution.py:526
  77.4 1.9 %copy.8 = bf16[512,512]{1,0:T(8,128)(2,1)} copy(bf16[512,512]{1,0:T(8,128)(2,1)} %ring_attention.1) | data formatting | bytes 1048576

commit v4 on v3

--- a/solution.py
+++ b/solution.py
@@ -146,9 +146,11 @@
     def send_own(half):
         for way in range(2):
             ring_copy(b, 0, half, way, 0).start()
+        sib_copy(b, 0, half, 0).start()
+
+    def send_swap(half):
         for which in range(2):
             swap(half, which).start()
-        sib_copy(b, 0, half, 0).start()
 
     def send_swapped(half):
         for which in range(2):
@@ -210,11 +212,13 @@
             )
             return carry
 
-        lax.fori_loop(0, 4, unit, 0)
+        lax.fori_loop(0, 4, unit, 0, unroll=True)
 
     diagonal(b, 0)
+    send_swap(0)
     send_own(1)
     swap_q.wait_recv()
+    send_swap(1)
     event(0, 1, 0)
 
     def w_copy(step):
@@ -429,6 +433,50 @@
         send_head(ob.at[0], 0, 0, 1, my_head, 2).start()
         for i, dy in enumerate((1, 3)):
             send_head(ob.at[0], dy, 0, 0, my_head, 3 + i).start()
+
+    @pl.when(c == 1)
+    def _():
+        for i, dy in enumerate(steps):
+            send_head(ob.at[0], dy, 0, 0, my_head, 3 + i).start()
+        for i, (e_hi, e_lo) in enumerate(others):
+            send_head(ob.at[e_hi], 0, e_hi, e_lo, my_head, 6 + i).start()
+
+    og[my_head] = ob[0]
+    for j in range(N_TENSOR):
+        w_sib_arrived(j)
+
+    for half in range(2):
+        for which in range(2):
+            swap(half, which).wait_send()
+    swap_q.wait_send()
+    for step in range(1, N_TENSOR):
+        w_copy(step).wait_send()
+    for step in range(N_TENSOR):
+        w_sib(step).wait_send()
+
+    def sent(i, carry):
+        part = i // 2
+        half = lax.rem(i, 2)
+
+        def sib_sent(distance, inner):
+            sib_copy(0, part, half, distance).wait_send()
+            return inner
+
+        lax.fori_loop(0, N_Z, sib_sent, 0)
+        for way in range(2):
+
+            def ring_sent(step, inner, way=way):
+                ring_copy(0, part, half, way, step).wait_send()
+                return inner
+
+            reach = 4 - part if way == 0 else 3 + part
+            lax.fori_loop(0, reach, ring_sent, 0)
+        return carry
+
+    lax.fori_loop(0, 4, sent, 0)
+
+    @pl.when(c == 0)
+    def _():
         lanes = ((0, 0), (0, 1), (1, 1), (1, 0))
         for k, (e_hi, e_lo) in enumerate(lanes):
             if k > 0:
@@ -444,10 +492,6 @@
 
     @pl.when(c == 1)
     def _():
-        for i, dy in enumerate(steps):
-            send_head(ob.at[0], dy, 0, 0, my_head, 3 + i).start()
-        for i, (e_hi, e_lo) in enumerate(others):
-            send_head(ob.at[e_hi], 0, e_hi, e_lo, my_head, 6 + i).start()
         for k, dy in enumerate(steps):
             transit_arrived(dy)
             head = head_at(4 - dy, 0, 0)
@@ -456,11 +500,6 @@
             arrived(head)
             send_head(og.at[head], 0, 0, 1, head, 11 + 3 * k).start()
 
-    og[my_head] = ob[0]
-    for j in range(N_TENSOR):
-        w_sib_arrived(j)
-
-    total[...] = jnp.zeros_like(total)
     for dy in (0, 1, 3, 2):
         for e_lo in range(2):
             first = 4 * lax.rem(y + dy, 4) + 2 * lax.rem(x_lo + e_lo, 2)
@@ -474,17 +513,13 @@
                     pl.when(c == 1)(functools.partial(arrived, head))
             rows = jnp.concatenate([og[first], og[first + 1]], axis=1)
             weight = jnp.concatenate([wb[first], wb[first + 1]], axis=0)
-            total[...] += jnp.dot(rows, weight, preferred_element_type=jnp.float32)
-    out_ref[...] = total[...].astype(jnp.bfloat16)
-
-    for half in range(2):
-        for which in range(2):
-            swap(half, which).wait_send()
-    swap_q.wait_send()
-    for step in range(1, N_TENSOR):
-        w_copy(step).wait_send()
-    for step in range(N_TENSOR):
-        w_sib(step).wait_send()
+            product = jnp.dot(rows, weight, preferred_element_type=jnp.float32)
+            if (dy, e_lo) == (0, 0):
+                total[...] = product
+            elif (dy, e_lo) == (2, 1):
+                out_ref[...] = (total[...] + product).astype(jnp.bfloat16)
+            else:
+                total[...] += product
 
     def head_sent(index, carry):
         send_head(ob.at[0], 1, 0, 0, my_head, index).wait_send()
@@ -496,27 +531,6 @@
 
     lax.fori_loop(0, 11 + 7 * c, head_sent, 0)
     lax.fori_loop(0, 8 * (1 - c), relay_sent, 0)
-
-    def sent(i, carry):
-        part = i // 2
-        half = lax.rem(i, 2)
-
-        def sib_sent(distance, inner):
-            sib_copy(0, part, half, distance).wait_send()
-            return inner
-
-        lax.fori_loop(0, N_Z, sib_sent, 0)
-        for way in range(2):
-
-            def ring_sent(step, inner, way=way):
-                ring_copy(0, part, half, way, step).wait_send()
-                return inner
-
-            reach = 4 - part if way == 0 else 3 + part
-            lax.fori_loop(0, reach, ring_sent, 0)
-        return carry
-
-    lax.fori_loop(0, 4, sent, 0)
 
 
 def body(queries, key_states, value_states, out_weight, lengths, cycle_order):

time: 79.4 us -> 78.9 us (level)
  no operation moved by 1% of the time
where the time goes in v4:
time: 78.9 us; the launch traced here: 78.8 us
  Pallas kernels  76.9 us (97%)
  local copies, waits for them, and re-layouts  1.87 us (2%)
    pallas_call x1, Pallas kernels, body(): pl.pallas_call(kernel, out_shape=jax.ShapeDtypeStruct((CAP, CAP), jnp.bfl...  76.9 us
    unnamed x1, local copies, waits for them, and re-layouts  1.87 us

profile of v4, /device:TPU:1, one launch (start us, length us, event | category | flops | bytes accessed | tf_op | source)
XLA Modules:
  0.0 78.8 jit_solution(17785736381642199480)
XLA Ops:
  0.0 76.9 %ring_attention.1 = bf16[512,512]{1,0:T(8,128)(2,1)} custom-call(bf16[512,256]{1,0:T(8,128)(2,1)} %q_ref.1, bf16[512,256]{1,0:T(8,128)(2,1)} %k_ref.1, bf16[512,256]{1,0:T(8,128)(2,1)} %v_ref.1, bf16[256,4096]{1,0:T(8,128)(2,1)} %w_ref.1, s32[1,32]{1,0:T(1,128)} %bitcast.2, s32[1,32]{1,0:T(1,128)} %bitcast.3), custom_call_target="tpu_custom_call" | custom-call | tf_op jit(solution)/shard_map/ring_attention/pallas_call | solution.py:540
  76.9 1.9 %copy.8 = bf16[512,512]{1,0:T(8,128)(2,1)} copy(bf16[512,512]{1,0:T(8,128)(2,1)} %ring_attention.1) | data formatting | bytes 1048576

commit v5 on v4

--- a/solution.py
+++ b/solution.py
@@ -333,10 +333,6 @@
                 for j in range(N_TENSOR):
                     w_sib(j).start()
 
-            @pl.when((ph == 1) & (r == 8))
-            def _():
-                last_event(0)
-
             @pl.when(ph == 1)
             def _():
                 for half in range(2):
@@ -348,28 +344,38 @@
             attend(block_of(z + N_Z - s, side, core), block_of(z + s, side, core_y))
             return inner
 
-        lax.fori_loop(0, 2 - single - 2 * (s // 4), phase, 0)
+        lax.fori_loop(0, 2 - single, phase, 0)
         return carry
 
-    lax.fori_loop(1, 9, round_step, 0)
+    lax.fori_loop(1, 7, round_step, 0)
 
     def last_step(i, carry):
-        half = i // 2
+        far = i // 4
+        half = lax.rem(i // 2, 2)
         core = lax.rem(c + i, 2)
 
         @pl.when(i == 2)
         def _():
+            event(1, 3, 1)
+
+        @pl.when(i == 4)
+        def _():
+            last_event(0)
+
+        @pl.when(i == 6)
+        def _():
             last_event(1)
 
         @pl.when(lax.rem(i, 2) == 1)
         def _():
-            sib_wait(0, half, 4)
-            sib_wait(1, half, 4)
-
-        attend(block_of(z + 4, h, core), block_of(z + 4, 1 - h, core), half)
+            sib_wait(1 - far, half, 5 - far)
+            sib_wait(1, half, 3 + far)
+
+        side = lax.rem(h + 1 - far, 2)
+        attend(block_of(z + 5 - far, side, core), block_of(z + 3 + far, 1 - h, core), half)
         return carry
 
-    lax.fori_loop(0, 4, last_step, 0)
+    lax.fori_loop(0, 8, last_step, 0)
 
     def finish(half):
         for i in range(4):

time: 78.9 us -> 78.3 us (level)
  no operation moved by 1% of the time
where the time goes in v5:
time: 78.3 us; the launch traced here: 78.2 us
  Pallas kernels  76.3 us (97%)
  local copies, waits for them, and re-layouts  1.87 us (2%)
    pallas_call x1, Pallas kernels, body(): pl.pallas_call(kernel, out_shape=jax.ShapeDtypeStruct((CAP, CAP), jnp.bfl...  76.3 us
    unnamed x1, local copies, waits for them, and re-layouts  1.87 us

profile of v5, /device:TPU:1, one launch (start us, length us, event | category | flops | bytes accessed | tf_op | source)
XLA Modules:
  0.0 78.2 jit_solution(17685077783239352084)
XLA Ops:
  0.0 76.3 %ring_attention.1 = bf16[512,512]{1,0:T(8,128)(2,1)} custom-call(bf16[512,256]{1,0:T(8,128)(2,1)} %q_ref.1, bf16[512,256]{1,0:T(8,128)(2,1)} %k_ref.1, bf16[512,256]{1,0:T(8,128)(2,1)} %v_ref.1, bf16[256,4096]{1,0:T(8,128)(2,1)} %w_ref.1, s32[1,32]{1,0:T(1,128)} %bitcast.2, s32[1,32]{1,0:T(1,128)} %bitcast.3), custom_call_target="tpu_custom_call" | custom-call | tf_op jit(solution)/shard_map/ring_attention/pallas_call | solution.py:546
  76.3 1.9 %copy.8 = bf16[512,512]{1,0:T(8,128)(2,1)} copy(bf16[512,512]{1,0:T(8,128)(2,1)} %ring_attention.1) | data formatting | bytes 1048576

commit v6 on v5

--- a/solution.py
+++ b/solution.py
@@ -418,7 +418,7 @@
         remote(at, at, hs_s.at[0], h_r.at[half * 16 + head], partner).wait_recv()
 
     others = ((1, 0), (1, 1), (0, 1))
-    steps = (1, 3, 2)
+    near = (1, 3)
 
     finish(1)
 
@@ -429,8 +429,9 @@
 
     @pl.when(c == 1)
     def _():
-        for i, dy in enumerate(steps):
+        for i, dy in enumerate(near):
             send_transit(dy, i).start()
+        send_transit(2, 16).start()
 
     finish(0)
 
@@ -442,10 +443,10 @@
 
     @pl.when(c == 1)
     def _():
-        for i, dy in enumerate(steps):
-            send_head(ob.at[0], dy, 0, 0, my_head, 3 + i).start()
+        for i, dy in enumerate(near):
+            send_head(ob.at[0], dy, 0, 0, my_head, 2 + i).start()
         for i, (e_hi, e_lo) in enumerate(others):
-            send_head(ob.at[e_hi], 0, e_hi, e_lo, my_head, 6 + i).start()
+            send_head(ob.at[e_hi], 0, e_hi, e_lo, my_head, 4 + i).start()
 
     og[my_head] = ob[0]
     for j in range(N_TENSOR):
@@ -498,13 +499,18 @@
 
     @pl.when(c == 1)
     def _():
-        for k, dy in enumerate(steps):
+        for k, dy in enumerate((1, 3, 2)):
+            head = head_at(4 - dy, 0, 0)
             transit_arrived(dy)
-            head = head_at(4 - dy, 0, 0)
-            send_head(transit.at[dy - 1], 0, 1, 0, head, 9 + 3 * k).start()
-            send_head(transit.at[dy - 1], 0, 1, 1, head, 10 + 3 * k).start()
-            arrived(head)
-            send_head(og.at[head], 0, 0, 1, head, 11 + 3 * k).start()
+            send_head(transit.at[dy - 1], 0, 1, 0, head, 7 + 3 * k).start()
+            send_head(transit.at[dy - 1], 0, 1, 1, head, 8 + 3 * k).start()
+            if dy == 2:
+                half_arrived(0, head)
+                half_arrived(1, head)
+            else:
+                arrived(head)
+                send_half(k, dy, head, k).start()
+            send_head(og.at[head], 0, 0, 1, head, 9 + 3 * k).start()
 
     for dy in (0, 1, 3, 2):
         for e_lo in range(2):
@@ -535,8 +541,8 @@
         send_half(0, 1, my_head, index).wait_send()
         return carry
 
-    lax.fori_loop(0, 11 + 7 * c, head_sent, 0)
-    lax.fori_loop(0, 8 * (1 - c), relay_sent, 0)
+    lax.fori_loop(0, 11 + 6 * c, head_sent, 0)
+    lax.fori_loop(0, 8 - 6 * c, relay_sent, 0)
 
 
 def body(queries, key_states, value_states, out_weight, lengths, cycle_order):
@@ -568,7 +574,7 @@
             dma((32,)),
             dma((15,)),
             dma((15,)),
-            dma((18,)),
+            dma((17,)),
             dma((16,)),
             dma((3,)),
             dma((8,)),

time: 78.3 us -> 78.3 us (level)
  no operation moved by 1% of the time
where the time goes in v6:
time: 78.3 us; the launch traced here: 78.1 us
  Pallas kernels  76.3 us (97%)
  local copies, waits for them, and re-layouts  1.87 us (2%)
    pallas_call x1, Pallas kernels, body(): pl.pallas_call(kernel, out_shape=jax.ShapeDtypeStruct((CAP, CAP), jnp.bfl...  76.3 us
    unnamed x1, local copies, waits for them, and re-layouts  1.87 us

profile of v6, /device:TPU:1, one launch (start us, length us, event | category | flops | bytes accessed | tf_op | source)
XLA Modules:
  0.0 78.1 jit_solution(17158449670398729127)
XLA Ops:
  0.0 76.3 %ring_attention.1 = bf16[512,512]{1,0:T(8,128)(2,1)} custom-call(bf16[512,256]{1,0:T(8,128)(2,1)} %q_ref.1, bf16[512,256]{1,0:T(8,128)(2,1)} %k_ref.1, bf16[512,256]{1,0:T(8,128)(2,1)} %v_ref.1, bf16[256,4096]{1,0:T(8,128)(2,1)} %w_ref.1, s32[1,32]{1,0:T(1,128)} %bitcast.2, s32[1,32]{1,0:T(1,128)} %bitcast.3), custom_call_target="tpu_custom_call" | custom-call | tf_op jit(solution)/shard_map/ring_attention/pallas_call | solution.py:552
  76.3 1.9 %copy.8 = bf16[512,512]{1,0:T(8,128)(2,1)} copy(bf16[512,512]{1,0:T(8,128)(2,1)} %ring_attention.1) | data formatting | bytes 1048576

commit v7 on v6

--- a/solution.py
+++ b/solution.py
@@ -431,6 +431,8 @@
     def _():
         for i, dy in enumerate(near):
             send_transit(dy, i).start()
+        for i, (e_hi, e_lo) in enumerate(others[:2]):
+            send_head(ob.at[1], 0, e_hi, e_lo, my_head, 4 + i).start()
         send_transit(2, 16).start()
 
     finish(0)
@@ -445,8 +447,7 @@
     def _():
         for i, dy in enumerate(near):
             send_head(ob.at[0], dy, 0, 0, my_head, 2 + i).start()
-        for i, (e_hi, e_lo) in enumerate(others):
-            send_head(ob.at[e_hi], 0, e_hi, e_lo, my_head, 4 + i).start()
+        send_head(ob.at[0], 0, 0, 1, my_head, 6).start()
 
     og[my_head] = ob[0]
     for j in range(N_TENSOR):

time: 78.3 us -> 78.3 us (level)
  no operation moved by 1% of the time
where the time goes in v7:
time: 78.3 us; the launch traced here: 78.1 us
  Pallas kernels  76.2 us (97%)
  local copies, waits for them, and re-layouts  1.87 us (2%)
    pallas_call x1, Pallas kernels, body(): pl.pallas_call(kernel, out_shape=jax.ShapeDtypeStruct((CAP, CAP), jnp.bfl...  76.2 us
    unnamed x1, local copies, waits for them, and re-layouts  1.87 us

profile of v7, /device:TPU:1, one launch (start us, length us, event | category | flops | bytes accessed | tf_op | source)
XLA Modules:
  0.0 78.1 jit_solution(5528326144245195566)
XLA Ops:
  0.0 76.2 %ring_attention.1 = bf16[512,512]{1,0:T(8,128)(2,1)} custom-call(bf16[512,256]{1,0:T(8,128)(2,1)} %q_ref.1, bf16[512,256]{1,0:T(8,128)(2,1)} %k_ref.1, bf16[512,256]{1,0:T(8,128)(2,1)} %v_ref.1, bf16[256,4096]{1,0:T(8,128)(2,1)} %w_ref.1, s32[1,32]{1,0:T(1,128)} %bitcast.2, s32[1,32]{1,0:T(1,128)} %bitcast.3), custom_call_target="tpu_custom_call" | custom-call | tf_op jit(solution)/shard_map/ring_attention/pallas_call | solution.py:553
  76.2 1.9 %copy.8 = bf16[512,512]{1,0:T(8,128)(2,1)} copy(bf16[512,512]{1,0:T(8,128)(2,1)} %ring_attention.1) | data formatting | bytes 1048576
